TPU v7x, 256 devices: a whole 4x4x8 slice. The times are simulated.
256 devices in a mesh: seq: 32 (over y, z), mp: 8 (over x, core).
Axes of the slice: x: 4, y: 4, z: 8, core: 2. Of those that a mesh axis runs over, the one named last changes fastest.
Arguments:
- patch_hidden: bfloat16 [16384, 5120], P('seq', 'mp'), may hold values from -6 to 6
- out_weight: bfloat16 [5120, 8192], P(None, 'mp'), may hold values from -0.078125 to 0.078125
- out_bias: bfloat16 [8192], P('mp'), may hold values from -3 to 3
- cluster_ids: int32 [16384], P('seq'), may hold values from 0 to 8191, as said below
- memory_slots: bfloat16 [8192, 8192], P('seq', 'mp'), may hold values from -6 to 6
- slot_counts: int32 [8192], P('seq'), may hold values from 1 to 16
- norm_gain: bfloat16 [8192], P('mp'), may hold values from 0.099609375 to 1.8984375
- key_weight: bfloat16 [8192, 1024], P('seq', 'mp'), may hold values from -0.0625 to 0.0625
- value_weight: bfloat16 [8192, 1024], P('seq', 'mp'), may hold values from -0.0625 to 0.0625
- key_bias: bfloat16 [1024], P('mp'), may hold values from -3 to 3
- value_bias: bfloat16 [1024], P('mp'), may hold values from -3 to 3
Outputs:
- memory_new: bfloat16 [8192, 8192], P('seq', 'mp')
- slot_keys: bfloat16 [8192, 1024], P('seq', 'mp')
- slot_values: bfloat16 [8192, 1024], P('seq', 'mp')
Inputs may be any that keep to these rules, and one draw needn't show every extreme that they name: `cluster_ids`: slots s * 256 to (s + 1) * 256 - 1 belong to index s of seq. Of the 512 rows of one index of seq, at most 48 name slots of any one index of seq, and in every draw some index of seq receives exactly 48 rows from every index of seq.
All inputs are finite; a program needn't handle non-finite values.
Results may differ from a plain program's by a relative error of at most 0.0054.
Values may be sent and summed in bfloat16 or wider, within the bound.
A program may use at most 128 MiB of HBM per device.

v0:
```python
import jax
import jax.numpy as jnp
from jax import lax
from jax.sharding import PartitionSpec as P

D = 8192


def on_device(
    patch_hidden,
    out_weight,
    out_bias,
    cluster_ids,
    memory_slots,
    slot_counts,
    norm_gain,
    key_weight,
    value_weight,
    key_bias,
    value_bias,
):
    row_count = patch_hidden.shape[0]
    width_local = out_weight.shape[1]
    slot_local = memory_slots.shape[0]
    seq_count = lax.axis_size("seq")
    capacity = 3 * row_count // seq_count
    bias_wide = out_bias.astype(jnp.float32)
    owner = cluster_ids // slot_local
    owner_table = (owner[:, None] == jnp.arange(seq_count, dtype=jnp.int32)[None, :]).astype(
        jnp.int32
    )
    rank = jnp.sum(jnp.cumsum(owner_table, axis=0) * owner_table, axis=1) - 1
    target = owner * capacity + rank
    send_slots = (
        jnp.full((seq_count * capacity,), -1, jnp.int32).at[target].set(cluster_ids % slot_local)
    )
    activated = jax.nn.gelu(
        lax.all_gather(patch_hidden, "mp", axis=1, tiled=True).astype(jnp.float32),
        approximate=False,
    ).astype(jnp.bfloat16)
    projected = jnp.dot(activated, out_weight, preferred_element_type=jnp.float32)
    merged = projected + bias_wide[None, :]
    send_rows = jnp.zeros((seq_count * capacity, width_local), jnp.float32).at[target].set(merged)
    got_rows, got_slots = (
        lax.all_to_all(send_rows, "seq", split_axis=0, concat_axis=0, tiled=True),
        lax.all_to_all(send_slots, "seq", split_axis=0, concat_axis=0, tiled=True),
    )
    matches = jnp.arange(slot_local, dtype=jnp.int32)[:, None] == got_slots[None, :]
    totals = jnp.dot(
        matches.astype(jnp.float32),
        got_rows,
        precision=lax.Precision.HIGHEST,
        preferred_element_type=jnp.float32,
    )
    arrivals = jnp.sum(matches.astype(jnp.float32), axis=1)
    weight = slot_counts.astype(jnp.float32)
    memory_new = (
        (weight[:, None] * memory_slots.astype(jnp.float32) + totals) / (weight + arrivals)[:, None]
    ).astype(jnp.bfloat16)
    key_full, value_full = (
        lax.all_gather(key_weight, "seq", axis=0, tiled=True),
        lax.all_gather(value_weight, "seq", axis=0, tiled=True),
    )
    head_local = key_full.shape[1]
    stored = lax.optimization_barrier(memory_new).astype(jnp.float32)
    squares = lax.psum(jnp.sum(stored * stored, axis=1), "mp")
    inverse = lax.rsqrt(squares / D + 1e-06)
    normed = (stored * inverse[:, None] * norm_gain.astype(jnp.float32)[None, :]).astype(
        jnp.bfloat16
    )
    key_rows, value_rows = (
        lax.all_to_all(key_full, "mp", split_axis=0, concat_axis=1, tiled=True),
        lax.all_to_all(value_full, "mp", split_axis=0, concat_axis=1, tiled=True),
    )
    mp_count = key_rows.shape[1] // head_local
    joined = jnp.stack(
        [
            key_rows.reshape(width_local, mp_count, head_local),
            value_rows.reshape(width_local, mp_count, head_local),
        ],
        axis=2,
    ).reshape(width_local, 2 * mp_count * head_local)
    shared = lax.psum_scatter(
        lax.dot_general(
            joined, normed, (((0,), (1,)), ((), ())), preferred_element_type=jnp.float32
        ),
        "mp",
        scatter_dimension=0,
        tiled=True,
    )
    combined = shared.T
    key_part = combined[:, :head_local]
    value_part = combined[:, head_local:]
    slot_keys = (key_part + key_bias.astype(jnp.float32)[None, :]).astype(jnp.bfloat16)
    slot_values = (value_part + value_bias.astype(jnp.float32)[None, :]).astype(jnp.bfloat16)
    return (memory_new, slot_keys, slot_values)


def solution(mesh):
    return jax.shard_map(
        on_device,
        mesh=mesh,
        in_specs=(
            P("seq", "mp"),
            P(None, "mp"),
            P("mp"),
            P("seq"),
            P("seq", "mp"),
            P("seq"),
            P("mp"),
            P("seq", "mp"),
            P("seq", "mp"),
            P("mp"),
            P("mp"),
        ),
        out_specs=(P("seq", "mp"), P("seq", "mp"), P("seq", "mp")),
        check_vma=False,
    )
```

profile of v0, /device:TPU:8, one launch (start us, length us, event | category | flops | bytes accessed | tf_op | source)
XLA Modules:
  0.0 477.1 jit_solution(14380446403744334530)
XLA Ops:
  7.2 0.7 all-gather.8.cloned.1.call-update
  7.9 0.7 all-gather.6.cloned.1.call-update
  8.7 0.7 all-gather.4.cloned.1.call-update
  9.4 0.7 add_select_fusion
  10.1 1.2 reduce-window.6
  11.3 0.2 slice_reduce_fusion
  11.5 0.1 fusion.52
  11.6 2.5 scatter_custom_fusion
  14.2 20.1 %all_to_all.53 = s32[32,48,1]{1,2,0:T(1,128)S(1)} all-to-all(s32[32,48,1]{1,2,0:T(1,128)S(1)} %bitcast.39), channel_id=1, replica_groups=mesh['seq'=32,'mp'=8] {'seq'}, dimensions={0} | all-to-all | bytes 12288 | tf_op jit(solution)/shard_map/all_to_all | solution.py:46
  34.3 55.9 %all-gather.8.cloned.1.call-done = bf16[8192,128]{1,0:T(8,128)(2,1)} async-done(((bf16[256,128]{1,0:T(8,128)(2,1)}), bf16[8192,128]{1,0:T(8,128)(2,1)}) %all-gather.8.cloned.1.call-update) | async-done | bytes 2097168 | tf_op jit(solution)/shard_map/all_gather | solution.py:62
  90.2 4.3 all-to-all-start.3
  94.5 0.7 convert_element_type.53
  95.2 72.8 %all-gather.6.cloned.1.call-done = bf16[8192,128]{1,0:T(8,128)(2,1)} async-done(((bf16[256,128]{1,0:T(8,128)(2,1)}), bf16[8192,128]{1,0:T(8,128)(2,1)}) %all-gather.6.cloned.1.call-update) | async-done | bytes 2097168 | tf_op jit(solution)/shard_map/all_gather | solution.py:61
  168.0 4.4 all-to-all-start.2
  172.3 49.5 %all-gather.4.cloned.1.call-done = bf16[512,5120]{1,0:T(8,128)(2,1)} async-done(((bf16[512,640]{1,0:T(8,128)(2,1)}), bf16[512,5120]{1,0:T(8,128)(2,1)}) %all-gather.4.cloned.1.call-update) | async-done | bytes 5242896 | tf_op jit(solution)/shard_map/all_gather | solution.py:38
  221.8 31.9 %fusion.31 = f32[512,1024]{1,0:T(8,128)} fusion(bf16[5120,1024]{1,0:T(8,128)(2,1)} %param.12, bf16[512,5120]{1,0:T(8,128)(2,1)} %all-gather.4.cloned.1.call-done), kind=kOutput, calls=%fused_computation.36 | convolution fusion | flops 5541724160 | bytes 17825792 | tf_op jit(solution)/shard_map/dot_general | solution.py:41
  253.7 6.4 %scatter_custom_fusion.1 = f32[1536,1024]{1,0:T(8,128)} fusion(s32[512]{0:T(512)S(1)} %compare_select_fusion, f32[]{:T(128)} %constant.48.clone.1, f32[512,1024]{1,0:T(8,128)} %fusion.31, f32[1024]{0:T(1024)S(1)} %convert_element_type.53), kind=kCustom, calls=%fused_computation.38 | custom fusion | flops 524288 | bytes 8392708 | tf_op jit(solution)/shard_map/scatter | solution.py:43
  260.2 7.3 %all-to-all-start.1 = ((f32[32,48,1024]{2,1,0:T(8,128)}), f32[32,48,1024]{2,1,0:T(8,128)}, u32[]{:S(2)}, u32[]{:S(2)}) async-start(f32[32,48,1024]{2,1,0:T(8,128)} %bitcast.33), calls=%async_computation.1 | async-start | bytes 12582912 | tf_op jit(solution)/shard_map/all_to_all | solution.py:45
  267.6 0.5 broadcast.74
  268.1 0.7 reduce.5
  268.9 0.2 convert_reduce_fusion
  269.2 3.9 pad_maximum_fusion
  273.1 6.5 %copy.30 = bf16[1024,8,2,128]{0,3,2,1:T(8,128)(2,1)} copy(bf16[1024,8,2,128]{3,0,1,2:T(8,128)(2,1)} %pad_maximum_fusion) | data formatting | bytes 8388608 | tf_op jit(solution)/shard_map/stack | solution.py:76
  279.5 128.1 %all-to-all-done.1 = f32[32,48,1024]{2,1,0:T(8,128)} async-done(((f32[32,48,1024]{2,1,0:T(8,128)}), f32[32,48,1024]{2,1,0:T(8,128)}, u32[]{:S(2)}, u32[]{:S(2)}) %all-to-all-start.1) | async-done | bytes 6291488 | tf_op jit(solution)/shard_map/all_to_all | solution.py:45
  407.6 6.3 %fusion.39 = bf16[256,1024]{1,0:T(8,128)(2,1)S(1)} fusion(f32[1536,1024]{1,0:T(8,128)} %bitcast.4, bf16[256,1024]{1,0:T(8,128)(2,1)S(1)} %copy-done.3, s32[1536]{0:T(1024)S(1)} %eq.48, f32[256]{0:T(256)S(1)} %convert_add_fusion, f32[256]{0:T(256)S(1)} %convert_element_type.48), kind=kOutput, calls=%fused_computation.48 | convolution fusion | flops 4833542144 | bytes 7348224 | tf_op jit(solution)/shard_map/dot_general | solution.py:49
  413.9 0.2 fusion.40
  414.1 12.4 %psum.7 = f32[256]{0:T(256)S(1)} all-reduce(f32[256]{0:T(256)S(1)} %fusion.40), channel_id=1, replica_groups=mesh['seq'=32,'mp'=8] {'mp'}, use_global_device_ids=true, to_apply=%region_7.8 | all-reduce | flops 256 | bytes 2048 | tf_op jit(solution)/shard_map/psum | solution.py:66
  426.5 4.9 %fusion.45 = f32[2048,256]{1,0:T(8,128)} fusion(bf16[1024,2048]{0,1:T(8,128)(2,1)} %bitcast.35, bf16[256,1024]{1,0:T(8,128)(2,1)S(1)} %fusion.39, f32[1024]{0:T(1024)S(1)} %convert_element_type.57, f32[256]{0:T(256)S(1)} %add_rsqrt_fusion), kind=kOutput, calls=%fused_computation.54 | convolution fusion | flops 1074790400 | bytes 6820864 | tf_op jit(solution)/shard_map/dot_general | solution.py:84
  431.5 36.5 %reduce-scatter.2.cloned.1.call-done = f32[256,256]{1,0:T(8,128)} async-done(((f32[2048,256]{1,0:T(8,128)}), f32[256,256]{1,0:T(8,128)}) %reduce-scatter.2.cloned.1.call-update) | async-done | bytes 262160 | tf_op jit(solution)/shard_map/reduce_scatter | solution.py:83
  468.0 1.1 fusion.49
  469.1 0.7 copy.31
  469.8 0.7 copy.32
  (31 shorter events, 0.4 us)
Async XLA Ops:
  7.2 83.1 %all-gather.8.cloned.1.call-start = ((), (), s32[]{:S(2)}) async-start(), calls=%async_computation.7 | async-start | bytes 2162688 | tf_op jit(solution)/shard_map/all_gather | solution.py:62
  7.9 160.1 %all-gather.6.cloned.1.call-start = ((), (), s32[]{:S(2)}) async-start(), calls=%async_computation.6 | async-start | bytes 2162688 | tf_op jit(solution)/shard_map/all_gather | solution.py:61
  8.6 213.2 %all-gather.4.cloned.1.call-start = ((), (), s32[]{:S(2)}) async-start(), calls=%async_computation.5 | async-start | bytes 5898240 | tf_op jit(solution)/shard_map/all_gather | solution.py:38
  90.2 77.7 %all-to-all-start.3 = ((bf16[8,1024,128]{2,1,0:T(8,128)(2,1)}), bf16[8,1024,128]{2,1,0:T(8,128)(2,1)S(1)}, u32[]{:S(2)}, u32[]{:S(2)}) async-start(bf16[8,1024,128]{2,1,0:T(8,128)(2,1)} %bitcast.37), calls=%async_computation.3 | async-start | bytes 4194304 | tf_op jit(solution)/shard_map/all_to_all | solution.py:73
  168.0 92.2 %all-to-all-start.2 = ((bf16[8,1024,128]{2,1,0:T(8,128)(2,1)}), bf16[8,1024,128]{2,1,0:T(8,128)(2,1)}, u32[]{:S(2)}, u32[]{:S(2)}) async-start(bf16[8,1024,128]{2,1,0:T(8,128)(2,1)} %bitcast.36), calls=%async_computation.2 | async-start | bytes 4194304 | tf_op jit(solution)/shard_map/all_to_all | solution.py:72
  253.7 13.9 %copy-start.1 = (s32[256]{0:T(256)S(1)}, s32[256]{0:T(256)}, u32[]{:S(2)}) copy-start(s32[256]{0:T(256)} %param.16) | copy-start | bytes 3076
  253.7 13.9 %copy-start.2 = (bf16[1024]{0:T(1024)(128)(2,1)S(1)}, bf16[1024]{0:T(1024)(128)(2,1)}, u32[]{:S(2)}) copy-start(bf16[1024]{0:T(1024)(128)(2,1)} %param.17) | copy-start | bytes 6148
  260.2 147.4 %all-to-all-start.1 = ((f32[32,48,1024]{2,1,0:T(8,128)}), f32[32,48,1024]{2,1,0:T(8,128)}, u32[]{:S(2)}, u32[]{:S(2)}) async-start(f32[32,48,1024]{2,1,0:T(8,128)} %bitcast.33), calls=%async_computation.1 | async-start | bytes 12582912 | tf_op jit(solution)/shard_map/all_to_all | solution.py:45
  267.5 140.1 %copy-start.3 = (bf16[256,1024]{1,0:T(8,128)(2,1)S(1)}, bf16[256,1024]{1,0:T(8,128)(2,1)}, u32[]{:S(2)}) copy-start(bf16[256,1024]{1,0:T(8,128)(2,1)} %param.15) | copy-start | bytes 1572868
  267.5 200.5 %reduce-scatter.2.cloned.1.call-start = ((), (), s32[]{:S(2)}) async-start(), calls=%async_computation.8 | async-start | bytes 2359296 | tf_op jit(solution)/shard_map/reduce_scatter | solution.py:83
  279.5 151.9 %copy-start.4 = (bf16[128]{0:T(256)(128)(2,1)S(1)}, bf16[128]{0:T(256)(128)(2,1)}, u32[]{:S(2)}) copy-start(bf16[128]{0:T(256)(128)(2,1)} %param.21) | copy-start | bytes 772
  279.5 151.9 %copy-start.5 = (bf16[128]{0:T(256)(128)(2,1)S(1)}, bf16[128]{0:T(256)(128)(2,1)}, u32[]{:S(2)}) copy-start(bf16[128]{0:T(256)(128)(2,1)} %param.20) | copy-start | bytes 772
  413.9 56.7 %copy-start = (bf16[256,1024]{1,0:T(8,128)(2,1)}, bf16[256,1024]{1,0:T(8,128)(2,1)S(1)}, u32[]{:S(2)}) copy-start(bf16[256,1024]{1,0:T(8,128)(2,1)S(1)} %fusion.39) | copy-start | bytes 1572868
Sparse Core Ops, SparseCore 0:
  10.6 79.5 all-gather.7
  92.8 75.0 all-gather.5
  169.8 51.9 all-gather.3
  431.6 36.4 reduce-scatter.1
where the time goes:
time: 478 us; the launch traced here: 477 us
  waiting for transfers between devices  345 us (72%)
  matrix products  43.1 us (9%)
  blocking collectives  32.6 us (7%)
  starting transfers between devices  16.1 us (3%)
  other arithmetic  15.2 us (3%)
  between operations  13.9 us (3%)
  local copies, waits for them, and re-layouts  11.3 us (2%)
    all_to_all x1, waiting for transfers between devices, on_device(): lax.all_to_all(send_rows, 'seq', split_axis=0, concat_axis=0, tiled=True)  128 us
    all_gather x1, waiting for transfers between devices, on_device(): lax.all_gather(key_weight, 'seq', axis=0, tiled=True)  72.8 us
    all_gather x1, waiting for transfers between devices, on_device(): lax.all_gather(value_weight, 'seq', axis=0, tiled=True)  55.9 us
    all_gather x1, waiting for transfers between devices, on_device(): lax.all_gather(patch_hidden, 'mp', axis=1, tiled=True).astype(jnp.float32)  49.5 us
    reduce_scatter x1, waiting for transfers between devices, on_device(): lax.psum_scatter(lax.dot_general(joined, normed, (((0,), (1,)), ((), ()))...  36.5 us
    dot_general x1, matrix products, on_device(): jnp.dot(activated, out_weight, preferred_element_type=jnp.float32)  31.9 us
    all_to_all x1, blocking collectives, on_device(): lax.all_to_all(send_slots, 'seq', split_axis=0, concat_axis=0, tiled=True)  20.1 us
    psum x1, blocking collectives, on_device(): squares = lax.psum(jnp.sum(stored * stored, axis=1), 'mp')  12.4 us
  transfers between devices with their start and end apart: 7, of which 5 were waited for; matrix products, arithmetic and copies ran while one was open for 12% of the time, Pallas kernels for 0%

commit v1 on v0

--- a/solution.py
+++ b/solution.py
@@ -4,6 +4,11 @@
 from jax.sharding import PartitionSpec as P
 
 D = 8192
+
+
+def gather_by_exchange(x, axis, dim):
+    copies = jnp.concatenate([x] * lax.axis_size(axis), axis=dim)
+    return lax.all_to_all(copies, axis, dim, dim, tiled=True)
 
 
 def on_device(
@@ -58,7 +63,7 @@
         (weight[:, None] * memory_slots.astype(jnp.float32) + totals) / (weight + arrivals)[:, None]
     ).astype(jnp.bfloat16)
     key_full, value_full = (
-        lax.all_gather(key_weight, "seq", axis=0, tiled=True),
+        gather_by_exchange(key_weight, "seq", 0),
         lax.all_gather(value_weight, "seq", axis=0, tiled=True),
     )
     head_local = key_full.shape[1]

time: 478 us -> 431 us (0.902)
  waiting for transfers between devices: 345 us -> 262 us
  local copies, waits for them, and re-layouts: 11.3 us -> 41.1 us
  starting transfers between devices: 16.1 us -> 40.6 us
  blocking collectives: 32.6 us -> 13.7 us
    all_gather x1 -> x0, waiting for transfers between devices: 72.8 us -> none  [on_device(): lax.all_gather(key_weight, 'seq', axis=0, tiled=True)]
    all_gather x1, waiting for transfers between devices: 49.5 us -> 0.02 us  [on_device(): lax.all_gather(patch_hidden, 'mp', axis=1, tiled=True).astype(jnp.float32)]
    all_to_all x1, waiting for transfers between devices: 0.01 us -> 39.9 us  [on_device(): lax.all_to_all(value_full, 'mp', split_axis=0, concat_axis=1, tiled=True)]
    unnamed x14 -> x49, local copies, waits for them, and re-layouts: 1.49 us -> 30 us
    all_to_all x0 -> x2, waiting for transfers between devices: none -> 21.9 us  [the longest x1 21.9 us: gather_by_exchange(): return lax.all_to_all(copies, axis, dim, dim, tiled=True)]
    all_to_all x0 -> x2, starting transfers between devices: none -> 21.5 us  [the longest x1 11.7 us: on_device(): lax.all_to_all(send_slots, 'seq', split_axis=0, concat_axis=0, tiled=True)]
    all_to_all x1 -> x0, blocking collectives: 20.1 us -> none  [on_device(): lax.all_to_all(send_slots, 'seq', split_axis=0, concat_axis=0, tiled=True)]
    all_gather x1, waiting for transfers between devices: 55.9 us -> 35.9 us  [on_device(): lax.all_gather(value_weight, 'seq', axis=0, tiled=True)]
  transfers between devices with their start and end apart: 7 -> 8, of which waited for: 5 -> 5; matrix products, arithmetic and copies ran while one was open for 12% -> 20% of each run, Pallas kernels for 0% -> 0%
where the time goes in v1:
time: 431 us; the launch traced here: 430 us
  waiting for transfers between devices  262 us (61%)
  matrix products  43.3 us (10%)
  local copies, waits for them, and re-layouts  41.1 us (10%)
  starting transfers between devices  40.6 us (9%)
  other arithmetic  14.6 us (3%)
  between operations  14 us (3%)
  blocking collectives  13.7 us (3%)
    all_to_all x1, waiting for transfers between devices, on_device(): lax.all_to_all(send_rows, 'seq', split_axis=0, concat_axis=0, tiled=True)  128 us
    all_to_all x1, waiting for transfers between devices, on_device(): lax.all_to_all(value_full, 'mp', split_axis=0, concat_axis=1, tiled=True)  39.9 us
    all_gather x1, waiting for transfers between devices, on_device(): lax.all_gather(value_weight, 'seq', axis=0, tiled=True)  35.9 us
    reduce_scatter x1, waiting for transfers between devices, on_device(): lax.psum_scatter(lax.dot_general(joined, normed, (((0,), (1,)), ((), ()))...  34.9 us
    dot_general x1, matrix products, on_device(): jnp.dot(activated, out_weight, preferred_element_type=jnp.float32)  32.1 us
    unnamed x49, local copies, waits for them, and re-layouts  30 us
    all_to_all x1, waiting for transfers between devices, gather_by_exchange(): return lax.all_to_all(copies, axis, dim, dim, tiled=True)  21.9 us
    psum x1, blocking collectives, on_device(): squares = lax.psum(jnp.sum(stored * stored, axis=1), 'mp')  13.7 us
  transfers between devices with their start and end apart: 8, of which 5 were waited for; matrix products, arithmetic and copies ran while one was open for 20% of the time, Pallas kernels for 0%

profile of v1, /device:TPU:8, one launch (start us, length us, event | category | flops | bytes accessed | tf_op | source)
XLA Modules:
  0.0 429.7 jit_solution(9948198390956342205)
XLA Ops:
  8.6 1.2 reduce-window.6
  10.2 2.5 scatter_custom_fusion
  13.3 11.7 %all-to-all-start = ((s32[32,48,1]{1,2,0:T(1,128)}), s32[32,48,1]{1,2,0:T(1,128)S(1)}, u32[]{:S(2)}, u32[]{:S(2)}) async-start(s32[32,48,1]{1,2,0:T(1,128)} %bitcast.2), calls=%async_computation | async-start | bytes 32768 | tf_op jit(solution)/shard_map/all_to_all | solution.py:51
  25.8 1.5 constant_dynamic-update-slice_fusion.31
  27.2 1.5 constant_dynamic-update-slice_fusion.30
  28.7 1.5 constant_dynamic-update-slice_fusion.29
  30.2 1.5 constant_dynamic-update-slice_fusion.28
  31.6 1.5 constant_dynamic-update-slice_fusion.27
  33.1 1.5 constant_dynamic-update-slice_fusion.26
  34.5 1.5 constant_dynamic-update-slice_fusion.25
  36.0 1.5 constant_dynamic-update-slice_fusion.24
  37.5 1.5 constant_dynamic-update-slice_fusion.23
  38.9 1.5 constant_dynamic-update-slice_fusion.22
  40.4 1.5 constant_dynamic-update-slice_fusion.21
  54.9 9.8 %all-to-all-start.2 = ((bf16[32,256,128]{2,1,0:T(8,128)(2,1)}), bf16[32,256,128]{2,1,0:T(8,128)(2,1)}, u32[]{:S(2)}, u32[]{:S(2)}) async-start(bf16[32,256,128]{2,1,0:T(8,128)(2,1)} %bitcast.5), calls=%async_computation.2 | async-start | bytes 4194304 | tf_op jit(solution)/shard_map/all_to_all | solution.py:11
  64.8 35.9 %all-gather.5.cloned.1.call-done = bf16[8192,128]{1,0:T(8,128)(2,1)} async-done(((bf16[256,128]{1,0:T(8,128)(2,1)}), bf16[8192,128]{1,0:T(8,128)(2,1)}) %all-gather.5.cloned.1.call-update) | async-done | bytes 2097168 | tf_op jit(solution)/shard_map/all_gather | solution.py:67
  100.7 21.9 %all-to-all-done.2 = bf16[32,256,128]{2,1,0:T(8,128)(2,1)} async-done(((bf16[32,256,128]{2,1,0:T(8,128)(2,1)}), bf16[32,256,128]{2,1,0:T(8,128)(2,1)}, u32[]{:S(2)}, u32[]{:S(2)}) %all-to-all-start.2) | async-done | bytes 2097184 | tf_op jit(solution)/shard_map/all_to_all | solution.py:11
  122.6 4.3 all-to-all-start.4
  126.8 39.9 %all-to-all-done.4 = bf16[8,1024,128]{2,1,0:T(8,128)(2,1)S(1)} async-done(((bf16[8,1024,128]{2,1,0:T(8,128)(2,1)}), bf16[8,1024,128]{2,1,0:T(8,128)(2,1)S(1)}, u32[]{:S(2)}, u32[]{:S(2)}) %all-to-all-start.4) | async-done | bytes 2097184 | tf_op jit(solution)/shard_map/all_to_all | solution.py:78
  166.7 4.4 %all-to-all-start.3 = ((bf16[8,1024,128]{2,1,0:T(8,128)(2,1)}), bf16[8,1024,128]{2,1,0:T(8,128)(2,1)}, u32[]{:S(2)}, u32[]{:S(2)}) async-start(bf16[8,1024,128]{2,1,0:T(8,128)(2,1)} %bitcast.6), calls=%async_computation.3 | async-start | bytes 4194304 | tf_op jit(solution)/shard_map/all_to_all | solution.py:77
  171.1 32.1 %fusion.31 = f32[512,1024]{1,0:T(8,128)} fusion(bf16[5120,1024]{1,0:T(8,128)(2,1)} %param.12, bf16[512,5120]{1,0:T(8,128)(2,1)} %all-gather.3.cloned.1.call-done), kind=kOutput, calls=%fused_computation.36 | convolution fusion | flops 5541724160 | bytes 17825792 | tf_op jit(solution)/shard_map/dot_general | solution.py:46
  203.2 6.4 %scatter_custom_fusion.1 = f32[1536,1024]{1,0:T(8,128)} fusion(s32[512]{0:T(512)S(1)} %compare_select_fusion, f32[]{:T(128)} %constant.48.clone.1, f32[512,1024]{1,0:T(8,128)} %fusion.31, f32[1024]{0:T(1024)S(1)} %convert_element_type.53), kind=kCustom, calls=%fused_computation.38 | custom fusion | flops 524288 | bytes 8392708 | tf_op jit(solution)/shard_map/scatter | solution.py:48
  209.7 10.3 %all-to-all-start.1 = ((f32[32,48,1024]{2,1,0:T(8,128)}), f32[32,48,1024]{2,1,0:T(8,128)}, u32[]{:S(2)}, u32[]{:S(2)}) async-start(f32[32,48,1024]{2,1,0:T(8,128)} %bitcast.34), calls=%async_computation.1 | async-start | bytes 12582912 | tf_op jit(solution)/shard_map/all_to_all | solution.py:50
  221.6 3.9 pad_maximum_fusion
  225.5 6.5 %copy.30 = bf16[1024,8,2,128]{0,3,2,1:T(8,128)(2,1)} copy(bf16[1024,8,2,128]{3,0,1,2:T(8,128)(2,1)} %pad_maximum_fusion) | data formatting | bytes 8388608 | tf_op jit(solution)/shard_map/stack | solution.py:81
  232.1 128.5 %all-to-all-done.1 = f32[32,48,1024]{2,1,0:T(8,128)} async-done(((f32[32,48,1024]{2,1,0:T(8,128)}), f32[32,48,1024]{2,1,0:T(8,128)}, u32[]{:S(2)}, u32[]{:S(2)}) %all-to-all-start.1) | async-done | bytes 6291488 | tf_op jit(solution)/shard_map/all_to_all | solution.py:50
  360.5 6.3 %fusion.39 = bf16[256,1024]{1,0:T(8,128)(2,1)S(1)} fusion(f32[1536,1024]{1,0:T(8,128)} %bitcast.4, bf16[256,1024]{1,0:T(8,128)(2,1)S(1)} %copy-done.5, s32[1536]{0:T(1024)S(1)} %eq.48, f32[256]{0:T(256)S(1)} %convert_add_fusion, f32[256]{0:T(256)S(1)} %convert_element_type.48), kind=kOutput, calls=%fused_computation.48 | convolution fusion | flops 4833542144 | bytes 7348224 | tf_op jit(solution)/shard_map/dot_general | solution.py:54
  367.0 13.7 %psum.7 = f32[256]{0:T(256)S(1)} all-reduce(f32[256]{0:T(256)S(1)} %fusion.40), channel_id=1, replica_groups=mesh['seq'=32,'mp'=8] {'mp'}, use_global_device_ids=true, to_apply=%region_7.8 | all-reduce | flops 256 | bytes 2048 | tf_op jit(solution)/shard_map/psum | solution.py:71
  380.7 4.9 %fusion.45 = f32[2048,256]{1,0:T(8,128)} fusion(bf16[1024,2048]{0,1:T(8,128)(2,1)} %bitcast.36, bf16[256,1024]{1,0:T(8,128)(2,1)S(1)} %fusion.39, f32[1024]{0:T(1024)S(1)} %convert_element_type.57, f32[256]{0:T(256)S(1)} %add_rsqrt_fusion), kind=kOutput, calls=%fused_computation.54 | convolution fusion | flops 1074790400 | bytes 6820864 | tf_op jit(solution)/shard_map/dot_general | solution.py:89
  385.7 34.9 %reduce-scatter.2.cloned.1.call-done = f32[256,256]{1,0:T(8,128)} async-done(((f32[2048,256]{1,0:T(8,128)}), f32[256,256]{1,0:T(8,128)}) %reduce-scatter.2.cloned.1.call-update) | async-done | bytes 262160 | tf_op jit(solution)/shard_map/reduce_scatter | solution.py:88
  420.6 1.1 fusion.49
  421.7 0.7 copy.31
  (67 shorter events, 18.9 us)
Async XLA Ops:
  7.2 34.7 %copy-start = (bf16[256,128]{1,0:T(8,128)(2,1)S(1)}, bf16[256,128]{1,0:T(8,128)(2,1)}, u32[]{:S(2)}) copy-start(bf16[256,128]{1,0:T(8,128)(2,1)} %param.18) | copy-start | bytes 196612
  7.2 93.5 %all-gather.5.cloned.1.call-start = ((), (), s32[]{:S(2)}) async-start(), calls=%async_computation.7 | async-start | bytes 2162688 | tf_op jit(solution)/shard_map/all_gather | solution.py:67
  13.3 41.6 %all-to-all-start = ((s32[32,48,1]{1,2,0:T(1,128)}), s32[32,48,1]{1,2,0:T(1,128)S(1)}, u32[]{:S(2)}, u32[]{:S(2)}) async-start(s32[32,48,1]{1,2,0:T(1,128)} %bitcast.2), calls=%async_computation | async-start | bytes 32768 | tf_op jit(solution)/shard_map/all_to_all | solution.py:51
  25.0 146.1 %all-gather.3.cloned.1.call-start = ((), (), s32[]{:S(2)}) async-start(), calls=%async_computation.6 | async-start | bytes 5898240 | tf_op jit(solution)/shard_map/all_gather | solution.py:43
  54.9 67.7 %all-to-all-start.2 = ((bf16[32,256,128]{2,1,0:T(8,128)(2,1)}), bf16[32,256,128]{2,1,0:T(8,128)(2,1)}, u32[]{:S(2)}, u32[]{:S(2)}) async-start(bf16[32,256,128]{2,1,0:T(8,128)(2,1)} %bitcast.5), calls=%async_computation.2 | async-start | bytes 4194304 | tf_op jit(solution)/shard_map/all_to_all | solution.py:11
  64.8 62.1 %copy-start.3 = (bf16[1024]{0:T(1024)(128)(2,1)S(1)}, bf16[1024]{0:T(1024)(128)(2,1)}, u32[]{:S(2)}) copy-start(bf16[1024]{0:T(1024)(128)(2,1)} %param.13) | copy-start | bytes 6148
  122.6 44.2 %all-to-all-start.4 = ((bf16[8,1024,128]{2,1,0:T(8,128)(2,1)}), bf16[8,1024,128]{2,1,0:T(8,128)(2,1)S(1)}, u32[]{:S(2)}, u32[]{:S(2)}) async-start(bf16[8,1024,128]{2,1,0:T(8,128)(2,1)} %bitcast.37), calls=%async_computation.4 | async-start | bytes 4194304 | tf_op jit(solution)/shard_map/all_to_all | solution.py:78
  166.7 42.9 %all-to-all-start.3 = ((bf16[8,1024,128]{2,1,0:T(8,128)(2,1)}), bf16[8,1024,128]{2,1,0:T(8,128)(2,1)}, u32[]{:S(2)}, u32[]{:S(2)}) async-start(bf16[8,1024,128]{2,1,0:T(8,128)(2,1)} %bitcast.6), calls=%async_computation.3 | async-start | bytes 4194304 | tf_op jit(solution)/shard_map/all_to_all | solution.py:77
  209.7 10.4 %copy-start.2 = (s32[256]{0:T(256)S(1)}, s32[256]{0:T(256)}, u32[]{:S(2)}) copy-start(s32[256]{0:T(256)} %param.16) | copy-start | bytes 3076
  209.7 10.4 %copy-start.4 = (bf16[1024]{0:T(1024)(128)(2,1)S(1)}, bf16[1024]{0:T(1024)(128)(2,1)}, u32[]{:S(2)}) copy-start(bf16[1024]{0:T(1024)(128)(2,1)} %param.17) | copy-start | bytes 6148
  209.7 150.9 %all-to-all-start.1 = ((f32[32,48,1024]{2,1,0:T(8,128)}), f32[32,48,1024]{2,1,0:T(8,128)}, u32[]{:S(2)}, u32[]{:S(2)}) async-start(f32[32,48,1024]{2,1,0:T(8,128)} %bitcast.34), calls=%async_computation.1 | async-start | bytes 12582912 | tf_op jit(solution)/shard_map/all_to_all | solution.py:50
  220.0 200.6 %reduce-scatter.2.cloned.1.call-start = ((), (), s32[]{:S(2)}) async-start(), calls=%async_computation.8 | async-start | bytes 2359296 | tf_op jit(solution)/shard_map/reduce_scatter | solution.py:88
  225.5 135.0 %copy-start.5 = (bf16[256,1024]{1,0:T(8,128)(2,1)S(1)}, bf16[256,1024]{1,0:T(8,128)(2,1)}, u32[]{:S(2)}) copy-start(bf16[256,1024]{1,0:T(8,128)(2,1)} %param.15) | copy-start | bytes 1572868
  366.8 18.8 %copy-start.1 = (bf16[256,1024]{1,0:T(8,128)(2,1)}, bf16[256,1024]{1,0:T(8,128)(2,1)S(1)}, u32[]{:S(2)}) copy-start(bf16[256,1024]{1,0:T(8,128)(2,1)S(1)} %fusion.39) | copy-start | bytes 1572868
  380.7 5.0 %copy-start.6 = (bf16[128]{0:T(256)(128)(2,1)S(1)}, bf16[128]{0:T(256)(128)(2,1)}, u32[]{:S(2)}) copy-start(bf16[128]{0:T(256)(128)(2,1)} %param.21) | copy-start | bytes 772
  380.7 5.0 %copy-start.7 = (bf16[128]{0:T(256)(128)(2,1)S(1)}, bf16[128]{0:T(256)(128)(2,1)}, u32[]{:S(2)}) copy-start(bf16[128]{0:T(256)(128)(2,1)} %param.20) | copy-start | bytes 772
Sparse Core Ops, SparseCore 0:
  10.6 89.9 all-gather.4
  102.5 59.4 all-gather.2
  385.8 34.7 reduce-scatter.1
